TPU v7x, 32 devices: a whole 2x2x4 slice. The times are simulated.
32 devices in a mesh: tm: 4 (over y, x), space: 8 (over z, core).
Axes of the slice: x: 2, y: 2, z: 4, core: 2. Of those that a mesh axis runs over, the one named last changes fastest.
Arguments:
- frames: bfloat16 [4, 16, 96, 384], P('tm', 'space'), may hold values from -8 to 8
- cache_in: bfloat16 [2, 16, 96, 384], P(None, 'space'), may hold values from -6 to 6
- norm_gain: bfloat16 [384], replicated, may hold values from 0.5 to 1.5
- w_qkv: bfloat16 [384, 1152], replicated, may hold values from -0.5 to 0.5
- b_qkv: bfloat16 [1152], replicated, may hold values from -3 to 3
- w_proj: bfloat16 [384, 384], replicated, may hold values from -1.25 to 1.25
- b_proj: bfloat16 [384], replicated, may hold values from -2 to 2
- w_time: bfloat16 [3, 384, 768], replicated, may hold values from -0.1875 to 0.1875
- b_time: bfloat16 [768], replicated, may hold values from -3 to 3
- w_space: bfloat16 [3, 3, 384, 192], replicated, may hold values from -0.109375 to 0.109375
- b_space: bfloat16 [192], replicated, may hold values from -3 to 3
Outputs:
- decoded: bfloat16 [8, 32, 192, 192], P('tm', 'space')
All inputs are finite; a program needn't handle non-finite values.
Results may differ from a plain program's by a relative error of at most 0.01.
Values may be sent and summed in bfloat16 or wider, within the bound.
A program may use at most 64 MiB of HBM per device.

v0:
```python
import jax
import jax.numpy as jnp
from jax import lax
from jax.sharding import PartitionSpec as P

EPSILON = 1e-06


def shifted(value, axis, steps):
    count = lax.axis_size(axis)
    leading, last = (max(0, -steps), min(count, count - steps))
    return lax.ppermute(value, axis, [(source, source + steps) for source in range(leading, last)])


def with_halo(block, sides, width):
    for axis, dim in sides:
        count = lax.axis_size(axis)
        forward = [(i, i + 1) for i in range(count - 1)]
        backward = [(target, source) for source, target in forward]
        low = lax.ppermute(
            lax.slice_in_dim(block, block.shape[dim] - width, None, axis=dim), axis, forward
        )
        high = lax.ppermute(lax.slice_in_dim(block, 0, width, axis=dim), axis, backward)
        block = jnp.concatenate([low, block, high], axis=dim)
    return block


def normalize(frames, norm_gain):
    widened = frames.astype(jnp.float32)
    inverse = lax.rsqrt(jnp.mean(widened * widened, axis=-1, keepdims=True) + EPSILON)
    return (widened * inverse * norm_gain.astype(jnp.float32)).astype(jnp.bfloat16)


def project(rows, weight, bias):
    return (
        jnp.dot(rows, weight, preferred_element_type=jnp.float32) + bias.astype(jnp.float32)
    ).astype(jnp.bfloat16)


def attend(running, queries, key_rows, value_rows):
    best, mass, total_sum = running
    scores = lax.dot_general(
        queries, key_rows, (((1,), (1,)), ((), ())), preferred_element_type=jnp.float32
    ) * queries.shape[1] ** (-0.5)
    new_best = jnp.maximum(best, jnp.max(scores, axis=1, keepdims=True))
    weights = jnp.exp(scores - new_best)
    mass = jnp.sum(weights, axis=1, keepdims=True)
    total_sum = jnp.dot(
        weights.astype(jnp.bfloat16), value_rows, preferred_element_type=jnp.float32
    )
    return (new_best, mass, total_sum)


def body(
    frames, cache_in, norm_gain, w_qkv, b_qkv, w_proj, b_proj, w_time, b_time, w_space, b_space
):
    channels = frames.shape[-1]
    rows = frames.shape[1]
    width = frames.shape[2]
    normed = normalize(frames, norm_gain).reshape(-1, channels)
    queries = project(normed, w_qkv[:, :channels], b_qkv[:channels])
    count = queries.shape[0]
    start_state = (
        jnp.full((count, 1), -1e30, jnp.float32),
        jnp.zeros((count, 1), jnp.float32),
        jnp.zeros((count, channels), jnp.float32),
    )
    key_rows = project(normed, w_qkv[:, channels : 2 * channels], b_qkv[channels : 2 * channels])
    value_rows = project(normed, w_qkv[:, 2 * channels :], b_qkv[2 * channels :])
    final = attend(
        start_state,
        queries,
        lax.all_gather(key_rows, "space", axis=0, tiled=True),
        lax.all_gather(value_rows, "space", axis=0, tiled=True),
    )
    mixed = (final[2] / final[1]).astype(jnp.bfloat16)
    hidden = (
        frames.reshape(-1, channels).astype(jnp.float32)
        + jnp.dot(mixed, w_proj, preferred_element_type=jnp.float32)
        + b_proj.astype(jnp.float32)
    ).astype(jnp.bfloat16)
    position = lax.axis_index("tm")
    carried = cache_in.reshape(2, -1, channels)
    near_frame = shifted(hidden, "tm", 1)
    near_frame = jnp.where(position == 0, carried[1], near_frame)
    far_frame = shifted(near_frame, "tm", 1)
    far_frame = jnp.where(position == 0, carried[0], far_frame)
    timed = b_time.astype(jnp.float32) + jnp.dot(
        far_frame, w_time[0], preferred_element_type=jnp.float32
    )
    timed = timed + jnp.dot(near_frame, w_time[1], preferred_element_type=jnp.float32)
    timed = (timed + jnp.dot(hidden, w_time[2], preferred_element_type=jnp.float32)).astype(
        jnp.bfloat16
    )
    paired = jnp.stack([timed[:, :channels], timed[:, channels:]]).reshape(2, rows, width, channels)
    padded = with_halo(paired, (("space", 1),), 1)
    upsampled = jnp.repeat(jnp.repeat(padded, 2, axis=1)[:, 1 : 2 * rows + 3], 2, axis=2)
    upsampled = jnp.pad(upsampled, ((0, 0), (0, 0), (1, 1), (0, 0)))
    out_channels = w_space.shape[-1]
    result = jnp.zeros((8 * rows * width, out_channels), jnp.float32) + b_space.astype(jnp.float32)
    for row_tap in range(3):
        for col_tap in range(3):
            window = upsampled[
                :, row_tap : row_tap + 2 * rows, col_tap : col_tap + 2 * width
            ].reshape(-1, channels)
            result = result + jnp.dot(
                window, w_space[row_tap, col_tap], preferred_element_type=jnp.float32
            )
    return result.astype(jnp.bfloat16).reshape(2, 2 * rows, 2 * width, out_channels)


def solution(mesh):
    return jax.shard_map(
        body,
        mesh=mesh,
        in_specs=(
            P("tm", "space", None, None),
            P(None, "space", None, None),
            P(),
            P(),
            P(),
            P(),
            P(),
            P(),
            P(),
            P(),
            P(),
        ),
        out_specs=P("tm", "space", None, None),
        check_vma=False,
    )
```

profile of v0, /device:TPU:5, one launch (start us, length us, event | category | flops | bytes accessed | tf_op | source)
XLA Modules:
  0.0 114.7 jit_solution(11239914669437490637)
XLA Ops:
  6.5 0.0 all-gather.3.cloned.1.call-start
  6.6 1.1 multiply_reduce_fusion
  7.7 0.7 convert_element_type.64
  8.4 0.8 slice_convert_fusion.2
  9.2 1.0 multiply_convert_fusion
  10.2 1.9 %fusion.6 = bf16[192,384]{1,0:T(8,128)(2,1)} fusion(bf16[192,384]{1,0:T(8,128)(2,1)S(1)} %bitcast.88, bf16[384,1152]{1,0:T(8,128)(2,1)} %param.14, f32[384]{0:T(512)S(1)} %get-tuple-element.22), kind=kOutput, calls=%fused_computation.23 | convolution fusion | flops 56770560 | bytes 591360 | tf_op jit(solution)/shard_map/dot_general | solution.py:36
  12.1 0.0 all-gather.3.cloned.1.call-update
  12.1 0.0 all-gather.5.cloned.1.call-start
  12.2 0.9 fusion.7
  13.1 0.0 all-gather.5.cloned.1.call-update
  13.1 0.0 copy-done.7
  13.2 0.0 copy-done.5
  13.2 0.7 fusion.50
  13.9 22.7 %all-gather.3.cloned.1.call-done = bf16[1536,384]{1,0:T(8,128)(2,1)} async-done(((bf16[192,384]{1,0:T(8,128)(2,1)}), bf16[1536,384]{1,0:T(8,128)(2,1)}) %all-gather.3.cloned.1.call-update) | async-done | bytes 1179664 | tf_op jit(solution)/shard_map/all_gather | solution.py:73
  36.5 2.1 %fusion.51 = (f32[192]{0:T(256)S(1)}, f32[192,1536]{1,0:T(8,128)S(1)}) fusion(bf16[1536,384]{1,0:T(8,128)(2,1)} %all-gather.3.cloned.1.call-done, bf16[192,384]{1,0:T(8,128)(2,1)S(1)} %bitcast.90, bf16[384,1152]{1,0:T(8,128)(2,1)S(1)} %copy-done.6, f32[384]{0:T(512)S(1)} %get-tuple-element.20), kind=kOutput, calls=%fused_computation.83 | convolution fusion | flops 283852608 | bytes 2804480 | tf_op jit(solution)/shard_map/dot_general | solution.py:42
  38.6 0.0 copy-start.3
  38.7 0.3 fusion.10
  39.0 21.7 %all-gather.5.cloned.1.call-done = bf16[1536,384]{1,0:T(8,128)(2,1)} async-done(((bf16[192,384]{1,0:T(8,128)(2,1)}), bf16[1536,384]{1,0:T(8,128)(2,1)}) %all-gather.5.cloned.1.call-update) | async-done | bytes 1179664 | tf_op jit(solution)/shard_map/all_gather | solution.py:74
  60.6 2.8 %fusion.8 = bf16[192,384]{1,0:T(8,128)(2,1)} fusion(bf16[384,384]{1,0:T(8,128)(2,1)S(1)} %copy-done, bf16[1536,384]{1,0:T(8,128)(2,1)} %all-gather.5.cloned.1.call-done, f32[192,1536]{1,0:T(8,128)S(1)} %get-tuple-element.24, f32[192]{0:T(256)S(1)} %broadcast_maximum_fusion, f32[384]{0:T(512)S(1)} %convert_element_type.74, f32[192]{0:T(256)S(1)} %fusion.10, ...), kind=kOutput, calls=%fused_computation.25 | convolution fusion | flops 284147712 | bytes 2952192 | tf_op jit(solution)/shard_map/dot_general | solution.py:79
  63.4 3.2 %collective-permute-start = (bf16[192,384]{1,0:T(8,128)(2,1)}, bf16[192,384]{1,0:T(8,128)(2,1)S(1)}, u32[]{:S(2)}, u32[]{:S(2)}) collective-permute-start(bf16[192,384]{1,0:T(8,128)(2,1)} %fusion.8), channel_id=1, source_target_pairs={{0,8},{8,16},{16,24},{1,9},{9,17},{17,25},{2,10},{10,18},{18,26},{... | collective-permute-start | bytes 442376 | tf_op jit(solution)/shard_map/ppermute | solution.py:12
  66.7 1.3 %fusion.14 = f32[192,768]{1,0:T(8,128)S(1)} fusion(bf16[192,384]{1,0:T(8,128)(2,1)} %fusion.8, bf16[3,384,768]{2,1,0:T(8,128)(2,1)S(1)} %copy-done.1), kind=kOutput, calls=%fused_computation.36 | convolution fusion | flops 113246208 | bytes 1327104 | tf_op jit(solution)/shard_map/dot_general | solution.py:92
  67.9 3.8 %collective-permute-done = bf16[192,384]{1,0:T(8,128)(2,1)S(1)} collective-permute-done((bf16[192,384]{1,0:T(8,128)(2,1)}, bf16[192,384]{1,0:T(8,128)(2,1)S(1)}, u32[]{:S(2)}, u32[]{:S(2)}) %collective-permute-start) | collective-permute-done | bytes 147488 | tf_op jit(solution)/shard_map/ppermute | solution.py:12
  71.8 2.2 %collective-permute-start.1 = (bf16[192,384]{1,0:T(8,128)(2,1)S(1)}, bf16[192,384]{1,0:T(8,128)(2,1)S(1)}, u32[]{:S(2)}, u32[]{:S(2)}) collective-permute-start(bf16[192,384]{1,0:T(8,128)(2,1)S(1)} %bitcast_select_fusion), channel_id=1, source_target_pairs={{0,8},{8,16},{16,24},{1,9},{9,17},{17,25},{2,10},{10,18},{18,26},{... | collective-permute-start | bytes 442376 | tf_op jit(solution)/shard_map/ppermute | solution.py:12
  74.0 0.3 fusion.16
  74.3 4.3 %collective-permute-done.1 = bf16[192,384]{1,0:T(8,128)(2,1)S(1)} collective-permute-done((bf16[192,384]{1,0:T(8,128)(2,1)S(1)}, bf16[192,384]{1,0:T(8,128)(2,1)S(1)}, u32[]{:S(2)}, u32[]{:S(2)}) %collective-permute-start.1) | collective-permute-done | bytes 147488 | tf_op jit(solution)/shard_map/ppermute | solution.py:12
  78.6 0.0 copy-start.9
  78.6 0.3 fusion.3
  79.0 5.3 %collective-permute-start.2 = (bf16[2,1,96,384]{3,2,1,0:T(8,128)(2,1)S(1)}, bf16[2,1,96,384]{3,2,1,0:T(8,128)(2,1)S(1)}, u32[]{:S(2)}, u32[]{:S(2)}) collective-permute-start(bf16[2,1,96,384]{3,2,1,0:T(8,128)(2,1)S(1)} %get-tuple-element.14), channel_id=1, source_target_pairs={{0,1},{1,2},{2,3},{3,4},{4,5},{5,6},{6,7},{8,9},{9,10},{10,11},{11... | collective-permute-start | bytes 442376 | tf_op jit(solution)/shard_map/ppermute | solution.py:20
  84.3 1.9 %collective-permute-start.3 = (bf16[2,1,96,384]{3,2,1,0:T(8,128)(2,1)S(1)}, bf16[2,1,96,384]{3,2,1,0:T(8,128)(2,1)S(1)}, u32[]{:S(2)}, u32[]{:S(2)}) collective-permute-start(bf16[2,1,96,384]{3,2,1,0:T(8,128)(2,1)S(1)} %get-tuple-element.15), channel_id=1, source_target_pairs={{1,0},{2,1},{3,2},{4,3},{5,4},{6,5},{7,6},{9,8},{10,9},{11,10},{12... | collective-permute-start | bytes 442376 | tf_op jit(solution)/shard_map/ppermute | solution.py:23
  86.3 0.1 collective-permute-done.2
  86.4 4.4 %collective-permute-done.3 = bf16[2,1,96,384]{3,2,1,0:T(8,128)(2,1)S(1)} collective-permute-done((bf16[2,1,96,384]{3,2,1,0:T(8,128)(2,1)S(1)}, bf16[2,1,96,384]{3,2,1,0:T(8,128)(2,1)S(1)}, u32[]{:S(2)}, u32[]{:S(2)}) %collective-permute-start.3) | collective-permute-done | bytes 147488 | tf_op jit(solution)/shard_map/ppermute | solution.py:23
  90.8 0.1 pad_maximum_fusion
  90.9 0.1 broadcast_in_dim.7
  91.0 0.1 slice.145
  91.1 2.3 %broadcast_in_dim.8 = bf16[2,6,96,2,384]{4,3,2,1,0:T(2,128)(2,1)} broadcast(bf16[2,6,96,384]{3,2,1,0:T(8,128)(2,1)S(1)} %slice.145), dimensions={0,1,2,4} | broadcast | bytes 2654208 | tf_op jit(solution)/shard_map/broadcast_in_dim | solution.py:97
  93.4 4.0 %reshape.81 = bf16[2,6,192,384]{3,2,1,0:T(8,128)(2,1)S(1)} reshape(bf16[2,6,96,2,384]{4,3,2,1,0:T(2,128)(2,1)} %broadcast_in_dim.8) | data formatting | bytes 3538944 | tf_op jit(solution)/shard_map/reshape | solution.py:97
  97.4 0.0 copy-start.2
  97.4 4.0 %pad_slice_fusion = (bf16[2,4,192,384]{3,2,1,0:T(8,128)(2,1)S(1)}, bf16[2,4,192,384]{3,2,1,0:T(8,128)(2,1)S(1)}, bf16[2,4,192,384]{3,2,1,0:T(8,128)(2,1)S(1)}, b...) fusion(bf16[2,6,192,384]{3,2,1,0:T(8,128)(2,1)S(1)} %reshape.81), kind=kLoop, calls=%fused_computation.29 | loop fusion | bytes 15925248 | tf_op jit(solution)/shard_map/slice | solution.py:103
  101.5 0.6 convolution_add_fusion.8
  102.0 0.6 convolution_add_fusion.7
  102.6 0.6 convolution_add_fusion.6
  103.2 0.6 convolution_add_fusion.5
  103.8 0.6 convolution_add_fusion.4
  104.4 0.6 convolution_add_fusion.3
  105.0 0.6 convolution_add_fusion.2
  105.5 0.6 convolution_add_fusion.1
  106.1 0.6 fusion
  106.7 1.2 %copy.13 = bf16[1536,192]{1,0:T(8,128)(2,1)} copy(bf16[1536,192]{0,1:T(8,128)(2,1)S(1)} %fusion) | data formatting | bytes 1179648 | tf_op jit(solution)/shard_map/reshape | solution.py:109
  (24 shorter events, 0.2 us)
Async XLA Ops:
  6.5 54.1 %copy-start = (bf16[384,384]{1,0:T(8,128)(2,1)S(1)}, bf16[384,384]{1,0:T(8,128)(2,1)}, u32[]{:S(2)}) copy-start(bf16[384,384]{1,0:T(8,128)(2,1)} %param.16) | copy-start | bytes 884740
  6.5 5.6 %copy-start.6 = (bf16[384,1152]{1,0:T(8,128)(2,1)S(1)}, bf16[384,1152]{1,0:T(8,128)(2,1)}, u32[]{:S(2)}) copy-start(bf16[384,1152]{1,0:T(8,128)(2,1)} %param.14) | copy-start | bytes 2654212
  6.5 6.6 %copy-start.8 = (bf16[384]{0:T(512)(128)(2,1)S(1)}, bf16[384]{0:T(512)(128)(2,1)}, u32[]{:S(2)}) copy-start(bf16[384]{0:T(512)(128)(2,1)} %param.17) | copy-start | bytes 2308
  6.5 6.6 %copy-start.7 = (bf16[768]{0:T(1024)(128)(2,1)S(1)}, bf16[768]{0:T(1024)(128)(2,1)}, u32[]{:S(2)}) copy-start(bf16[768]{0:T(1024)(128)(2,1)} %param.19) | copy-start | bytes 4612
  6.5 6.6 %copy-start.5 = (bf16[2,2,96,384]{3,2,1,0:T(8,128)(2,1)S(1)}, bf16[2,2,96,384]{3,2,1,0:T(8,128)(2,1)}, u32[]{:S(2)}) copy-start(bf16[2,2,96,384]{3,2,1,0:T(8,128)(2,1)} %param.12) | copy-start | bytes 884740
  6.5 30.0 %all-gather.3.cloned.1.call-start = ((), (), s32[]{:S(2)}) async-start(), calls=%async_computation | async-start | bytes 1327104 | tf_op jit(solution)/shard_map/all_gather | solution.py:73
  12.1 48.5 %all-gather.5.cloned.1.call-start = ((), (), s32[]{:S(2)}) async-start(), calls=%async_computation.1 | async-start | bytes 1327104 | tf_op jit(solution)/shard_map/all_gather | solution.py:74
  38.6 22.0 %copy-start.3 = (bf16[1,2,96,384]{3,2,1,0:T(8,128)(2,1)S(1)}, bf16[1,2,96,384]{3,2,1,0:T(8,128)(2,1)}, u32[]{:S(2)}) copy-start(bf16[1,2,96,384]{3,2,1,0:T(8,128)(2,1)} %param.11) | copy-start | bytes 442372
  60.6 6.0 %copy-start.1 = (bf16[3,384,768]{2,1,0:T(8,128)(2,1)S(1)}, bf16[3,384,768]{2,1,0:T(8,128)(2,1)}, u32[]{:S(2)}) copy-start(bf16[3,384,768]{2,1,0:T(8,128)(2,1)} %param.18) | copy-start | bytes 5308420
  63.4 8.3 %copy-start.4 = (bf16[1,2,96,384]{3,2,1,0:T(8,128)(2,1)S(1)}, bf16[1,2,96,384]{3,2,1,0:T(8,128)(2,1)}, u32[]{:S(2)}) copy-start(bf16[1,2,96,384]{3,2,1,0:T(8,128)(2,1)} %get-tuple-element.19) | copy-start | bytes 442372
  63.4 8.3 %collective-permute-start = (bf16[192,384]{1,0:T(8,128)(2,1)}, bf16[192,384]{1,0:T(8,128)(2,1)S(1)}, u32[]{:S(2)}, u32[]{:S(2)}) collective-permute-start(bf16[192,384]{1,0:T(8,128)(2,1)} %fusion.8), channel_id=1, source_target_pairs={{0,8},{8,16},{16,24},{1,9},{9,17},{17,25},{2,10},{10,18},{18,26},{... | collective-permute-start | bytes 442376 | tf_op jit(solution)/shard_map/ppermute | solution.py:12
  71.8 6.8 %collective-permute-start.1 = (bf16[192,384]{1,0:T(8,128)(2,1)S(1)}, bf16[192,384]{1,0:T(8,128)(2,1)S(1)}, u32[]{:S(2)}, u32[]{:S(2)}) collective-permute-start(bf16[192,384]{1,0:T(8,128)(2,1)S(1)} %bitcast_select_fusion), channel_id=1, source_target_pairs={{0,8},{8,16},{16,24},{1,9},{9,17},{17,25},{2,10},{10,18},{18,26},{... | collective-permute-start | bytes 442376 | tf_op jit(solution)/shard_map/ppermute | solution.py:12
  78.6 7.7 %copy-start.9 = (bf16[192]{0:T(256)(128)(2,1)S(1)}, bf16[192]{0:T(256)(128)(2,1)}, u32[]{:S(2)}) copy-start(bf16[192]{0:T(256)(128)(2,1)} %param.21) | copy-start | bytes 1156
  79.0 7.4 %collective-permute-start.2 = (bf16[2,1,96,384]{3,2,1,0:T(8,128)(2,1)S(1)}, bf16[2,1,96,384]{3,2,1,0:T(8,128)(2,1)S(1)}, u32[]{:S(2)}, u32[]{:S(2)}) collective-permute-start(bf16[2,1,96,384]{3,2,1,0:T(8,128)(2,1)S(1)} %get-tuple-element.14), channel_id=1, source_target_pairs={{0,1},{1,2},{2,3},{3,4},{4,5},{5,6},{6,7},{8,9},{9,10},{10,11},{11... | collective-permute-start | bytes 442376 | tf_op jit(solution)/shard_map/ppermute | solution.py:20
  84.3 6.5 %collective-permute-start.3 = (bf16[2,1,96,384]{3,2,1,0:T(8,128)(2,1)S(1)}, bf16[2,1,96,384]{3,2,1,0:T(8,128)(2,1)S(1)}, u32[]{:S(2)}, u32[]{:S(2)}) collective-permute-start(bf16[2,1,96,384]{3,2,1,0:T(8,128)(2,1)S(1)} %get-tuple-element.15), channel_id=1, source_target_pairs={{1,0},{2,1},{3,2},{4,3},{5,4},{6,5},{7,6},{9,8},{10,9},{11,10},{12... | collective-permute-start | bytes 442376 | tf_op jit(solution)/shard_map/ppermute | solution.py:23
  97.4 4.0 %copy-start.2 = (bf16[3,3,384,192]{2,3,1,0:T(8,128)(2,1)S(1)}, bf16[3,3,384,192]{2,3,1,0:T(8,128)(2,1)}, u32[]{:S(2)}) copy-start(bf16[3,3,384,192]{2,3,1,0:T(8,128)(2,1)} %param.20) | copy-start | bytes 3981316
Sparse Core Ops, SparseCore 0:
  12.2 24.2 all-gather.2
  38.2 22.4 all-gather.4
where the time goes:
time: 115 us
  waiting for transfers between devices  56.9 us (49%)
  matrix products  14.7 us (13%)
  between operations  13.7 us (12%)
  starting transfers between devices  12.7 us (11%)
  local copies, waits for them, and re-layouts  12.4 us (11%)
  other arithmetic  4.16 us (4%)
    all_gather x1, waiting for transfers between devices, body(): lax.all_gather(key_rows, 'space', axis=0, tiled=True)  22.7 us
    all_gather x1, waiting for transfers between devices, body(): lax.all_gather(value_rows, 'space', axis=0, tiled=True)  21.7 us
    ppermute x2, waiting for transfers between devices, shifted(): lax.ppermute(value, axis, [(source, source + steps) for source in range(l...  8.06 us
    ppermute x2, starting transfers between devices, shifted(): lax.ppermute(value, axis, [(source, source + steps) for source in range(l...  5.4 us
    ppermute x1, starting transfers between devices, with_halo(): lax.ppermute(lax.slice_in_dim(block, block.shape[dim] - width, None, axis...  5.3 us
    dot_general x9, matrix products, body(): jnp.dot(window, w_space[row_tap, col_tap], preferred_element_type=jnp.flo...  5.18 us
    ppermute x1, waiting for transfers between devices, with_halo(): lax.ppermute(lax.slice_in_dim(block, 0, width, axis=dim), axis, backward)  4.38 us
    slice x1, local copies, waits for them, and re-layouts, body(): upsampled[:, row_tap:row_tap + 2 * rows, col_tap:col_tap + 2 * width]  4 us
  transfers between devices with their start and end apart: 6, of which 6 were waited for; matrix products, arithmetic and copies ran while one was open for 5% of the time, Pallas kernels for 0%

commit v1 on v0

v1 whole, which is shorter than its diff:
```python
import functools

import jax
import jax.numpy as jnp
from jax import lax
from jax.experimental import pallas as pl
from jax.experimental.pallas import tpu as pltpu
from jax.sharding import PartitionSpec as P

EPSILON = 1e-06
F32 = jnp.float32
BF16 = jnp.bfloat16
MESH = pl.DeviceIdType.MESH


def mm(left, right):
    return jnp.dot(left, right, preferred_element_type=F32)


def mm_t(left, right):
    return lax.dot_general(left, right, (((1,), (1,)), ((), ())), preferred_element_type=F32)


def row_of(ref, start, size):
    return ref[...].astype(F32).reshape(1, -1)[:, start : start + size]


def kernel(
    chips, steps,
    frames, cache, gain, wqkv_h, bqkv, wproj_h, bproj, wtime_h, btime, wspace_h, bspace,
    out_h,
    xg, wqkv, wproj, wtime, wspace, wf, qp, best, mass, total, hid, hist, tacc, tim, halo, abuf,
    wide, outv,
    wsem, grecv, gsend, trecv, tsend, hrecv, hsend, osem,
):
    ch = frames.shape[-1]
    width = frames.shape[2]
    rows = 2 * width
    c2 = wspace.shape[-1]
    t = lax.axis_index("tm")
    s = lax.axis_index("space")
    z, c = s // 2, s % 2
    has_lo, has_hi = z > 0, z < chips - 1
    sib = z * 2 + (1 - c)

    loads = [
        pltpu.make_async_copy(src, dst, wsem.at[i])
        for i, (src, dst) in enumerate(
            ((wqkv_h, wqkv), (wspace_h, wspace), (wproj_h, wproj), (wtime_h, wtime))
        )
    ]
    for load in loads:
        load.start()

    barrier = pltpu.get_barrier_semaphore()
    cross = jnp.where(c == 0, s - 1, s + 1)
    has_cross = jnp.where(c == 0, has_lo, has_hi)
    peers = [
        (has_lo, t, s - 2),
        (has_hi, t, s + 2),
        (has_cross, t, cross),
        (t >= 1, t - 1, s),
        (t >= 2, t - 2, s),
        (t < steps - 1, t + 1, s),
        (t < steps - 2, t + 2, s),
    ]
    pl.semaphore_signal(barrier, inc=1, device_id=(t, sib), device_id_type=MESH)
    greeted = jnp.int32(1)
    for there, pt, ps in peers:
        greeted = greeted + there.astype(jnp.int32)

        @pl.when(there)
        def _(pt=pt, ps=ps):
            pl.semaphore_signal(barrier, inc=1, device_id=(pt, ps), device_id_type=MESH)

    for r in range(2):
        value = frames[0, r].astype(F32)
        inverse = lax.rsqrt(jnp.mean(value * value, axis=-1, keepdims=True) + EPSILON)
        xg[z, c, pl.ds(r * width, width), :] = (value * inverse * row_of(gain, 0, ch)).astype(BF16)

    pl.semaphore_wait(barrier, greeted)

    def block(origin, core, h, kind, target):
        piece = xg.at[origin, core, pl.ds(h * width, width), :]
        return pltpu.make_async_remote_copy(
            src_ref=piece,
            dst_ref=piece,
            send_sem=gsend.at[origin, h, kind],
            recv_sem=grecv.at[origin, core, h],
            device_id=(t, target),
            device_id_type=MESH,
        )

    for h in range(2):
        @pl.when(has_hi)
        def _(h=h):
            block(z, c, h, 0, s + 2).start()

        @pl.when(has_lo)
        def _(h=h):
            block(z, c, h, 2, s - 2).start()

        block(z, c, h, 1, sib).start()

    loads[0].wait()
    mine = xg[z, c]
    queries = (mm(mine, wqkv[:, :ch]) + row_of(bqkv, 0, ch)).astype(BF16)
    scale = ch ** (-0.5)
    qp[...] = (mm_t(queries, wqkv[:, ch : 2 * ch]) * scale).astype(BF16)
    offset = jnp.sum(queries.astype(F32) * row_of(bqkv, ch, ch), axis=1, keepdims=True) * scale

    def scores_of(origin):
        keys = xg[origin].reshape(2 * rows, ch)
        return keys, mm_t(qp[...], keys) + offset

    loads[1].wait()
    groups = (((0,), (1, 2)), ((0, 1), (2,)))
    for pr in range(2):
        for pc in range(2):
            for dr in range(2):
                for dc in range(2):
                    part = None
                    for i in groups[pr][dr]:
                        for j in groups[pc][dc]:
                            tap = wspace[i, j].astype(F32)
                            part = tap if part is None else part + tap
                    at = pl.ds((2 * dr + dc) * ch, ch)
                    wf[pr, pc, at, :] = jnp.concatenate(
                        [part, jnp.zeros((ch, 256 - c2), F32)], axis=1
                    ).astype(BF16)

    for h in range(2):
        block(z, 1 - c, h, 1, sib).wait_recv()
    keys, scores = scores_of(z)
    top = jnp.max(scores, axis=1, keepdims=True)
    weights = jnp.exp(scores - top)
    best[...] = top
    mass[...] = jnp.sum(weights, axis=1, keepdims=True)
    total[...] = mm(weights.astype(BF16), keys)

    def absorb(origin):
        keys, scores = scores_of(origin)
        top = jnp.maximum(best[...], jnp.max(scores, axis=1, keepdims=True))
        weights = jnp.exp(scores - top)
        shrink = jnp.exp(best[...] - top)
        best[...] = top
        mass[...] = mass[...] * shrink + jnp.sum(weights, axis=1, keepdims=True)
        total[...] = total[...] * shrink + mm(weights.astype(BF16), keys)

    @pl.loop(1, chips)
    def _(d):
        sides = (
            (z - d, z - d >= 0, has_hi, s + 2),
            (z + d, z + d <= chips - 1, has_lo, s - 2),
        )
        for h in range(2):
            for origin, there, onward, target in sides:
                @pl.when(there)
                def _(origin=origin, onward=onward, target=target, h=h):
                    block(origin, c, h, 1, sib).wait_recv()

                    @pl.when(onward)
                    def _():
                        block(origin, c, h, 0, target).start()

                    block(origin, c, h, 1, sib).start()

        for origin, there, onward, target in sides:
            @pl.when(there)
            def _(origin=origin):
                for h in range(2):
                    block(origin, 1 - c, h, 1, sib).wait_recv()
                absorb(origin)

    loads[2].wait()

    def passed(h, kind, target):
        return pltpu.make_async_remote_copy(
            src_ref=hid.at[h],
            dst_ref=hist.at[kind, h],
            send_sem=tsend.at[kind, h],
            recv_sem=trecv.at[kind, h],
            device_id=(target, s),
            device_id_type=MESH,
        )

    for h in range(2):
        at = pl.ds(h * width, width)
        rows_mixed = (total[at, :] / mass[at, :]).astype(BF16)
        mixed = (mm(rows_mixed, wqkv[:, 2 * ch :]) + row_of(bqkv, 2 * ch, ch)).astype(BF16)
        hid[h] = (
            frames[0, h].astype(F32) + mm(mixed, wproj[...]) + row_of(bproj, 0, ch)
        ).astype(BF16)

        @pl.when(t < steps - 1)
        def _(h=h):
            passed(h, 1, t + 1).start()

        @pl.when(t < steps - 2)
        def _(h=h):
            passed(h, 0, t + 2).start()

    @pl.when(t == 0)
    def _():
        hist[0] = cache[0]
        hist[1] = cache[1]

    @pl.when(t == 1)
    def _():
        hist[0] = cache[1]

    loads[3].wait()
    tacc[...] = mm(hid[...].reshape(rows, ch), wtime[2]) + row_of(btime, 0, 2 * ch)

    first = lax.broadcasted_iota(jnp.int32, (width, ch), 0) == 0
    final = lax.broadcasted_iota(jnp.int32, (width, ch), 0) == width - 1

    def spread(index, row):
        for f in range(2):
            value = row[:, f * ch : (f + 1) * ch]
            wider = value.astype(F32)
            abuf[index, f, :, :ch] = jnp.where(first, 0.0, pltpu.roll(wider, 1, 0)).astype(BF16)
            abuf[index, f, :, ch : 2 * ch] = value
            abuf[index, f, :, 2 * ch :] = jnp.where(
                final, 0.0, pltpu.roll(wider, width - 1, 0)
            ).astype(BF16)

    n_space = 2 * chips

    def edge(r, target):
        return pltpu.make_async_remote_copy(
            src_ref=tim.at[r],
            dst_ref=halo.at[1 - r],
            send_sem=hsend.at[r],
            recv_sem=hrecv.at[1 - r],
            device_id=(t, target),
            device_id_type=MESH,
        )

    for r in range(2):
        @pl.when(t >= 1)
        def _(r=r):
            passed(r, 1, t - 1).wait_recv()

        @pl.when(t >= 2)
        def _(r=r):
            passed(r, 0, t - 2).wait_recv()

        row = (
            tacc[pl.ds(r * width, width), :] + mm(hist[1, r], wtime[1]) + mm(hist[0, r], wtime[0])
        ).astype(BF16)
        tim[r] = row
        goes = (s > 0) if r == 0 else (s < n_space - 1)

        @pl.when(goes)
        def _(r=r):
            edge(r, s - 1 if r == 0 else s + 1).start()

        spread(1 + r, row)

    def convolve(j):
        upper, pr = ((0, 0), (1, 1), (1, 0), (2, 1))[j]
        for pc in range(2):
            value = jnp.concatenate([row_of(bspace, 0, c2), jnp.zeros((1, 256 - c2), F32)], axis=1)
            for dr in range(2):
                lhs = abuf[upper + dr, :, :, pc * ch : (pc + 2) * ch].reshape(rows, 2 * ch)
                value = value + mm(lhs, wf[pr, pc, 2 * dr * ch : 2 * (dr + 1) * ch, :])
            for half in range(2):
                for f in range(2):
                    wide[half, f, pl.ds(pc, width, stride=2), :] = value[
                        f * width : (f + 1) * width, half * 128 : (half + 1) * 128
                    ]
        for f in range(2):
            outv[j, f, :, :128] = wide[0, f].astype(BF16)
            outv[j, f, :, 128:] = wide[1, f, :, : c2 - 128].astype(BF16)

    def give(j):
        return pltpu.make_async_copy(outv.at[j], out_h.at[:, j], osem.at[j])

    for j in (1, 2):
        convolve(j)
        give(j).start()

    for side in range(2):
        comes = (s > 0) if side == 0 else (s < n_space - 1)

        @pl.when(comes)
        def _(side=side):
            edge(1 - side, s - 1 if side == 0 else s + 1).wait_recv()

        @pl.when(jnp.logical_not(comes))
        def _(side=side):
            halo[side] = jnp.zeros(halo.shape[1:], BF16)

        spread(3 * side, halo[side])
        convolve(3 * side)
        give(3 * side).start()

    for h in range(2):
        @pl.when(has_hi)
        def _(h=h):
            block(z, c, h, 0, s + 2).wait_send()

        @pl.when(has_lo)
        def _(h=h):
            block(z, c, h, 2, s - 2).wait_send()

        block(z, c, h, 1, sib).wait_send()

    @pl.loop(1, chips)
    def _(d):
        for h in range(2):
            for origin, there, onward, target in (
                (z - d, z - d >= 0, has_hi, s + 2),
                (z + d, z + d <= chips - 1, has_lo, s - 2),
            ):
                @pl.when(there)
                def _(origin=origin, onward=onward, target=target, h=h):
                    @pl.when(onward)
                    def _():
                        block(origin, c, h, 0, target).wait_send()

                    block(origin, c, h, 1, sib).wait_send()

    for h in range(2):
        @pl.when(t < steps - 1)
        def _(h=h):
            passed(h, 1, t + 1).wait_send()

        @pl.when(t < steps - 2)
        def _(h=h):
            passed(h, 0, t + 2).wait_send()

    @pl.when(s > 0)
    def _():
        edge(0, s - 1).wait_send()

    @pl.when(s < n_space - 1)
    def _():
        edge(1, s + 1).wait_send()

    for j in range(4):
        give(j).wait()


def solution(mesh):
    chips, steps = mesh.shape["space"] // 2, mesh.shape["tm"]

    def body(frames, cache, gain, wqkv, bqkv, wproj, bproj, wtime, btime, wspace, bspace):
        _, _, width, ch = frames.shape
        c2 = wspace.shape[-1]
        cache = cache.reshape((2,) + frames.shape[1:])
        rows = 2 * width
        vmem = pl.BlockSpec(memory_space=pltpu.VMEM)
        away = pl.BlockSpec(memory_space=pl.ANY)
        dma = pltpu.SemaphoreType.DMA
        return pl.pallas_call(
            functools.partial(kernel, chips, steps),
            out_shape=jax.ShapeDtypeStruct((2, 4, 2 * width, c2), BF16),
            in_specs=[vmem, vmem, vmem, away, vmem, away, vmem, away, vmem, away, vmem],
            out_specs=away,
            scratch_shapes=[
                pltpu.VMEM((chips, 2, rows, ch), BF16),
                pltpu.VMEM(wqkv.shape, BF16),
                pltpu.VMEM(wproj.shape, BF16),
                pltpu.VMEM(wtime.shape, BF16),
                pltpu.VMEM(wspace.shape, BF16),
                pltpu.VMEM((2, 2, 4 * ch, 256), BF16),
                pltpu.VMEM((rows, ch), BF16),
                pltpu.VMEM((rows, 1), F32),
                pltpu.VMEM((rows, 1), F32),
                pltpu.VMEM((rows, ch), F32),
                pltpu.VMEM((2, width, ch), BF16),
                pltpu.VMEM((2, 2, width, ch), BF16),
                pltpu.VMEM((rows, 2 * ch), F32),
                pltpu.VMEM((2, width, 2 * ch), BF16),
                pltpu.VMEM((2, width, 2 * ch), BF16),
                pltpu.VMEM((4, 2, width, 3 * ch), BF16),
                pltpu.VMEM((2, 2, 2 * width, 128), F32),
                pltpu.VMEM((4, 2, 2 * width, c2), BF16),
                dma((4,)),
                dma((chips, 2, 2)),
                dma((chips, 2, 3)),
                dma((2, 2)),
                dma((2, 2)),
                dma((2,)),
                dma((2,)),
                dma((4,)),
            ],
            compiler_params=pltpu.CompilerParams(
                collective_id=0, has_side_effects=True, vmem_limit_bytes=56 * 2**20
            ),
            cost_estimate=pl.CostEstimate(
                flops=2 * 10**9, bytes_accessed=6 * 10**6, transcendentals=300000
            ),
        )(frames, cache, gain, wqkv, bqkv, wproj, bproj, wtime, btime, wspace, bspace)

    return jax.shard_map(
        body,
        mesh=mesh,
        in_specs=(P("tm", "space", None, None), P(None, "space", None, None)) + (P(),) * 9,
        out_specs=P("tm", "space", None, None),
        check_vma=False,
    )
```

time: 115 us -> 37.5 us (0.33)
  the two profiles are of different devices: /device:TPU:5 before, /device:TPU:12 now
where the time goes in v1:
time: 37.5 us; the launch traced here: 37.3 us
  Pallas kernels  31.5 us (84%)
  local copies, waits for them, and re-layouts  5.73 us (15%)
    pallas_call x1, Pallas kernels, body(): pl.pallas_call(functools.partial(kernel, chips, steps), out_shape=jax.Sha...  31.5 us
    unnamed x2, local copies, waits for them, and re-layouts  5.73 us

profile of v1, /device:TPU:12, one launch (start us, length us, event | category | flops | bytes accessed | tf_op | source)
XLA Modules:
  0.0 37.3 jit_solution(18361305894875965444)
XLA Ops:
  0.0 3.7 %copy.12.wspace_h = bf16[3,3,384,192]{3,2,1,0:T(8,128)(2,1)} copy(bf16[3,3,384,192]{2,3,1,0:T(8,128)(2,1)} %param.20) | data formatting | bytes 2654208 | tf_op args[9]
  3.7 31.5 %shard_map.109 = bf16[2,4,192,192]{3,2,1,0:T(8,128)(2,1)} custom-call(bf16[1,2,96,384]{3,2,1,0:T(8,128)(2,1)} %frames.1, bf16[2,2,96,384]{3,2,1,0:T(8,128)(2,1)} %cache.1, bf16[384]{0:T(512)(128)(2,1)} %gain.1, bf16[384,1152]{1,0:T(8,128)(2,1)} %wqkv_h.1, bf16[1152]{0:T(1024)(128)(2,1)} %bqkv.1, bf16[384,384]{1,0:T(8,128)(2,1)} %wproj_h.1, ...), custom_call_target="tpu_custom_call" | custom-call | flops 2000000000 | bytes 6000000 | tf_op jit(solution)/shard_map/pallas_call | solution.py:357
  35.2 2.1 %copy.14 = bf16[2,4,192,192]{3,2,1,0:T(8,128)(2,1)} copy(bf16[2,4,192,192]{3,2,1,0:T(8,128)(2,1)} %shard_map.109) | data formatting | bytes 1179648

commit v2 on v1

--- a/solution.py
+++ b/solution.py
@@ -36,7 +36,8 @@
     ch = frames.shape[-1]
     width = frames.shape[2]
     rows = 2 * width
-    c2 = wspace.shape[-1]
+    c2 = wspace.shape[2]
+    relay = steps == 4
     t = lax.axis_index("tm")
     s = lax.axis_index("space")
     z, c = s // 2, s % 2
@@ -113,6 +114,53 @@
         keys = xg[origin].reshape(2 * rows, ch)
         return keys, mm_t(qp[...], keys) + offset
 
+    for h in range(2):
+        block(z, 1 - c, h, 1, sib).wait_recv()
+    keys, scores = scores_of(z)
+    top = jnp.max(scores, axis=1, keepdims=True)
+    weights = jnp.exp(scores - top)
+    best[...] = top
+    mass[...] = jnp.sum(weights, axis=1, keepdims=True)
+    total[...] = mm(weights.astype(BF16), keys)
+
+    def absorb(origin):
+        keys, scores = scores_of(origin)
+        top = jnp.maximum(best[...], jnp.max(scores, axis=1, keepdims=True))
+        weights = jnp.exp(scores - top)
+        shrink = jnp.exp(best[...] - top)
+        best[...] = top
+        mass[...] = mass[...] * shrink + jnp.sum(weights, axis=1, keepdims=True)
+        total[...] = total[...] * shrink + mm(weights.astype(BF16), keys)
+
+    def sides_of(d):
+        return (
+            (z - d, z - d >= 0, has_hi, s + 2),
+            (z + d, z + d <= chips - 1, has_lo, s - 2),
+        )
+
+    def forward(d):
+        for h in range(2):
+            for origin, there, onward, target in sides_of(d):
+                @pl.when(there)
+                def _(origin=origin, onward=onward, target=target, h=h):
+                    block(origin, c, h, 1, sib).wait_recv()
+
+                    @pl.when(onward)
+                    def _():
+                        block(origin, c, h, 0, target).start()
+
+                    block(origin, c, h, 1, sib).start()
+
+    def take(d):
+        for origin, there, onward, target in sides_of(d):
+            @pl.when(there)
+            def _(origin=origin):
+                for h in range(2):
+                    block(origin, 1 - c, h, 1, sib).wait_recv()
+                absorb(origin)
+
+    forward(1)
+
     loads[1].wait()
     groups = (((0,), (1, 2)), ((0, 1), (2,)))
     for pr in range(2):
@@ -124,53 +172,16 @@
                         for j in groups[pc][dc]:
                             tap = wspace[i, j].astype(F32)
                             part = tap if part is None else part + tap
-                    at = pl.ds((2 * dr + dc) * ch, ch)
-                    wf[pr, pc, at, :] = jnp.concatenate(
-                        [part, jnp.zeros((ch, 256 - c2), F32)], axis=1
-                    ).astype(BF16)
-
-    for h in range(2):
-        block(z, 1 - c, h, 1, sib).wait_recv()
-    keys, scores = scores_of(z)
-    top = jnp.max(scores, axis=1, keepdims=True)
-    weights = jnp.exp(scores - top)
-    best[...] = top
-    mass[...] = jnp.sum(weights, axis=1, keepdims=True)
-    total[...] = mm(weights.astype(BF16), keys)
-
-    def absorb(origin):
-        keys, scores = scores_of(origin)
-        top = jnp.maximum(best[...], jnp.max(scores, axis=1, keepdims=True))
-        weights = jnp.exp(scores - top)
-        shrink = jnp.exp(best[...] - top)
-        best[...] = top
-        mass[...] = mass[...] * shrink + jnp.sum(weights, axis=1, keepdims=True)
-        total[...] = total[...] * shrink + mm(weights.astype(BF16), keys)
-
-    @pl.loop(1, chips)
+                    at = (2 * dr + dc) * ch
+                    wf[pr, pc, :c2, at : at + ch] = part.astype(BF16)
+            wf[pr, pc, c2:, :] = jnp.zeros((256 - c2, 4 * ch), BF16)
+
+    take(1)
+
+    @pl.loop(2, chips)
     def _(d):
-        sides = (
-            (z - d, z - d >= 0, has_hi, s + 2),
-            (z + d, z + d <= chips - 1, has_lo, s - 2),
-        )
-        for h in range(2):
-            for origin, there, onward, target in sides:
-                @pl.when(there)
-                def _(origin=origin, onward=onward, target=target, h=h):
-                    block(origin, c, h, 1, sib).wait_recv()
-
-                    @pl.when(onward)
-                    def _():
-                        block(origin, c, h, 0, target).start()
-
-                    block(origin, c, h, 1, sib).start()
-
-        for origin, there, onward, target in sides:
-            @pl.when(there)
-            def _(origin=origin):
-                for h in range(2):
-                    block(origin, 1 - c, h, 1, sib).wait_recv()
-                absorb(origin)
+        forward(d)
+        take(d)
 
     loads[2].wait()
 
@@ -184,6 +195,18 @@
             device_id_type=MESH,
         )
 
+    def relayed(h):
+        return pltpu.make_async_remote_copy(
+            src_ref=hist.at[0, h],
+            dst_ref=hist.at[1, h],
+            send_sem=tsend.at[1, h],
+            recv_sem=trecv.at[1, h],
+            device_id=(t - 1, s),
+            device_id_type=MESH,
+        )
+
+    sends_near = (t == 0) | (t == 2) if relay else t < steps - 1
+
     for h in range(2):
         at = pl.ds(h * width, width)
         rows_mixed = (total[at, :] / mass[at, :]).astype(BF16)
@@ -192,7 +215,7 @@
             frames[0, h].astype(F32) + mm(mixed, wproj[...]) + row_of(bproj, 0, ch)
         ).astype(BF16)
 
-        @pl.when(t < steps - 1)
+        @pl.when(sends_near)
         def _(h=h):
             passed(h, 1, t + 1).start()
 
@@ -238,13 +261,18 @@
         )
 
     for r in range(2):
+        @pl.when(t >= 2)
+        def _(r=r):
+            passed(r, 0, t - 2).wait_recv()
+
+        if relay:
+            @pl.when(t == 3)
+            def _(r=r):
+                relayed(r).start()
+
         @pl.when(t >= 1)
         def _(r=r):
             passed(r, 1, t - 1).wait_recv()
-
-        @pl.when(t >= 2)
-        def _(r=r):
-            passed(r, 0, t - 2).wait_recv()
 
         row = (
             tacc[pl.ds(r * width, width), :] + mm(hist[1, r], wtime[1]) + mm(hist[0, r], wtime[0])
@@ -264,7 +292,7 @@
             value = jnp.concatenate([row_of(bspace, 0, c2), jnp.zeros((1, 256 - c2), F32)], axis=1)
             for dr in range(2):
                 lhs = abuf[upper + dr, :, :, pc * ch : (pc + 2) * ch].reshape(rows, 2 * ch)
-                value = value + mm(lhs, wf[pr, pc, 2 * dr * ch : 2 * (dr + 1) * ch, :])
+                value = value + mm_t(lhs, wf[pr, pc, :, 2 * dr * ch : 2 * (dr + 1) * ch])
             for half in range(2):
                 for f in range(2):
                     wide[half, f, pl.ds(pc, width, stride=2), :] = value[
@@ -323,13 +351,19 @@
                     block(origin, c, h, 1, sib).wait_send()
 
     for h in range(2):
-        @pl.when(t < steps - 1)
+        @pl.when(sends_near)
         def _(h=h):
             passed(h, 1, t + 1).wait_send()
 
         @pl.when(t < steps - 2)
         def _(h=h):
             passed(h, 0, t + 2).wait_send()
+
+    if relay:
+        @pl.when(t == 3)
+        def _():
+            for h in range(2):
+                relayed(h).wait_send()
 
     @pl.when(s > 0)
     def _():
@@ -349,6 +383,7 @@
     def body(frames, cache, gain, wqkv, bqkv, wproj, bproj, wtime, btime, wspace, bspace):
         _, _, width, ch = frames.shape
         c2 = wspace.shape[-1]
+        wspace = jnp.swapaxes(wspace, 2, 3)
         cache = cache.reshape((2,) + frames.shape[1:])
         rows = 2 * width
         vmem = pl.BlockSpec(memory_space=pltpu.VMEM)
@@ -365,7 +400,7 @@
                 pltpu.VMEM(wproj.shape, BF16),
                 pltpu.VMEM(wtime.shape, BF16),
                 pltpu.VMEM(wspace.shape, BF16),
-                pltpu.VMEM((2, 2, 4 * ch, 256), BF16),
+                pltpu.VMEM((2, 2, 256, 4 * ch), BF16),
                 pltpu.VMEM((rows, ch), BF16),
                 pltpu.VMEM((rows, 1), F32),
                 pltpu.VMEM((rows, 1), F32),

time: 37.5 us -> 35.3 us (0.941)
  local copies, waits for them, and re-layouts: 5.73 us -> 2.06 us
  Pallas kernels: 31.5 us -> 33 us
    unnamed x2 -> x1, local copies, waits for them, and re-layouts: 5.73 us -> 2.06 us
    pallas_call x1, Pallas kernels: 31.5 us -> 33 us  [body(): pl.pallas_call(functools.partial(kernel, chips, steps), out_shape=jax.Sha...]
where the time goes in v2:
time: 35.3 us; the launch traced here: 35.1 us
  Pallas kernels  33 us (93%)
  local copies, waits for them, and re-layouts  2.06 us (6%)
    pallas_call x1, Pallas kernels, body(): pl.pallas_call(functools.partial(kernel, chips, steps), out_shape=jax.Sha...  33 us
    unnamed x1, local copies, waits for them, and re-layouts  2.06 us

profile of v2, /device:TPU:12, one launch (start us, length us, event | category | flops | bytes accessed | tf_op | source)
XLA Modules:
  0.0 35.1 jit_solution(7301702367323539746)
XLA Ops:
  0.0 33.0 %shard_map.109 = bf16[2,4,192,192]{3,2,1,0:T(8,128)(2,1)} custom-call(bf16[1,2,96,384]{3,2,1,0:T(8,128)(2,1)} %frames.1, bf16[2,2,96,384]{3,2,1,0:T(8,128)(2,1)} %cache.1, bf16[384]{0:T(512)(128)(2,1)} %gain.1, bf16[384,1152]{1,0:T(8,128)(2,1)} %wqkv_h.1, bf16[1152]{0:T(1024)(128)(2,1)} %bqkv.1, bf16[384,384]{1,0:T(8,128)(2,1)} %wproj_h.1, ...), custom_call_target="tpu_custom_call" | custom-call | flops 2000000000 | bytes 6000000 | tf_op jit(solution)/shard_map/pallas_call | solution.py:392
  33.1 2.1 %copy.13 = bf16[2,4,192,192]{3,2,1,0:T(8,128)(2,1)} copy(bf16[2,4,192,192]{3,2,1,0:T(8,128)(2,1)} %shard_map.109) | data formatting | bytes 1179648

commit v3 on v2

--- a/solution.py
+++ b/solution.py
@@ -31,13 +31,12 @@
     out_h,
     xg, wqkv, wproj, wtime, wspace, wf, qp, best, mass, total, hid, hist, tacc, tim, halo, abuf,
     wide, outv,
-    wsem, grecv, gsend, trecv, tsend, hrecv, hsend, osem,
+    wsem, grecv, gsend, trecv, tsend, hrecv, hsend, osem, csem,
 ):
     ch = frames.shape[-1]
     width = frames.shape[2]
     rows = 2 * width
     c2 = wspace.shape[2]
-    relay = steps == 4
     t = lax.axis_index("tm")
     s = lax.axis_index("space")
     z, c = s // 2, s % 2
@@ -52,6 +51,18 @@
     ]
     for load in loads:
         load.start()
+
+    def cached(source, slot):
+        return pltpu.make_async_copy(cache.at[source], hist.at[slot], csem.at[slot])
+
+    @pl.when(t == 0)
+    def _():
+        cached(0, 0).start()
+        cached(1, 1).start()
+
+    @pl.when(t == 1)
+    def _():
+        cached(1, 0).start()
 
     barrier = pltpu.get_barrier_semaphore()
     cross = jnp.where(c == 0, s - 1, s + 1)
@@ -195,18 +206,6 @@
             device_id_type=MESH,
         )
 
-    def relayed(h):
-        return pltpu.make_async_remote_copy(
-            src_ref=hist.at[0, h],
-            dst_ref=hist.at[1, h],
-            send_sem=tsend.at[1, h],
-            recv_sem=trecv.at[1, h],
-            device_id=(t - 1, s),
-            device_id_type=MESH,
-        )
-
-    sends_near = (t == 0) | (t == 2) if relay else t < steps - 1
-
     for h in range(2):
         at = pl.ds(h * width, width)
         rows_mixed = (total[at, :] / mass[at, :]).astype(BF16)
@@ -215,7 +214,7 @@
             frames[0, h].astype(F32) + mm(mixed, wproj[...]) + row_of(bproj, 0, ch)
         ).astype(BF16)
 
-        @pl.when(sends_near)
+        @pl.when(t < steps - 1)
         def _(h=h):
             passed(h, 1, t + 1).start()
 
@@ -225,12 +224,12 @@
 
     @pl.when(t == 0)
     def _():
-        hist[0] = cache[0]
-        hist[1] = cache[1]
+        cached(0, 0).wait()
+        cached(1, 1).wait()
 
     @pl.when(t == 1)
     def _():
-        hist[0] = cache[1]
+        cached(1, 0).wait()
 
     loads[3].wait()
     tacc[...] = mm(hid[...].reshape(rows, ch), wtime[2]) + row_of(btime, 0, 2 * ch)
@@ -264,11 +263,6 @@
         @pl.when(t >= 2)
         def _(r=r):
             passed(r, 0, t - 2).wait_recv()
-
-        if relay:
-            @pl.when(t == 3)
-            def _(r=r):
-                relayed(r).start()
 
         @pl.when(t >= 1)
         def _(r=r):
@@ -351,19 +345,13 @@
                     block(origin, c, h, 1, sib).wait_send()
 
     for h in range(2):
-        @pl.when(sends_near)
+        @pl.when(t < steps - 1)
         def _(h=h):
             passed(h, 1, t + 1).wait_send()
 
         @pl.when(t < steps - 2)
         def _(h=h):
             passed(h, 0, t + 2).wait_send()
-
-    if relay:
-        @pl.when(t == 3)
-        def _():
-            for h in range(2):
-                relayed(h).wait_send()
 
     @pl.when(s > 0)
     def _():
@@ -375,6 +363,18 @@
 
     for j in range(4):
         give(j).wait()
+
+
+def handed_on(source, target, sem):
+    moves = [
+        pltpu.make_async_copy(source.at[f, j], target.at[f, j], sem.at[f, j])
+        for f in range(2)
+        for j in range(4)
+    ]
+    for move in moves:
+        move.start()
+    for move in moves:
+        move.wait()
 
 
 def solution(mesh):
@@ -389,10 +389,10 @@
         vmem = pl.BlockSpec(memory_space=pltpu.VMEM)
         away = pl.BlockSpec(memory_space=pl.ANY)
         dma = pltpu.SemaphoreType.DMA
-        return pl.pallas_call(
+        made = pl.pallas_call(
             functools.partial(kernel, chips, steps),
             out_shape=jax.ShapeDtypeStruct((2, 4, 2 * width, c2), BF16),
-            in_specs=[vmem, vmem, vmem, away, vmem, away, vmem, away, vmem, away, vmem],
+            in_specs=[vmem, away, vmem, away, vmem, away, vmem, away, vmem, away, vmem],
             out_specs=away,
             scratch_shapes=[
                 pltpu.VMEM((chips, 2, rows, ch), BF16),
@@ -421,6 +421,7 @@
                 dma((2,)),
                 dma((2,)),
                 dma((4,)),
+                dma((2,)),
             ],
             compiler_params=pltpu.CompilerParams(
                 collective_id=0, has_side_effects=True, vmem_limit_bytes=56 * 2**20
@@ -429,6 +430,14 @@
                 flops=2 * 10**9, bytes_accessed=6 * 10**6, transcendentals=300000
             ),
         )(frames, cache, gain, wqkv, bqkv, wproj, bproj, wtime, btime, wspace, bspace)
+        return pl.pallas_call(
+            handed_on,
+            out_shape=jax.ShapeDtypeStruct(made.shape, BF16),
+            in_specs=[away],
+            out_specs=away,
+            scratch_shapes=[dma((2, 4))],
+            compiler_params=pltpu.CompilerParams(vmem_limit_bytes=60 * 2**20),
+        )(made)
 
     return jax.shard_map(
         body,

time: 35.3 us -> 56.8 us (1.61)
  Pallas kernels: 33 us -> 56.6 us
  local copies, waits for them, and re-layouts: 2.06 us -> 0 us
    pallas_call x0 -> x1, Pallas kernels: none -> 25 us  [body(): pl.pallas_call(handed_on, out_shape=jax.ShapeDtypeStruct(made.shape, BF16...]
    unnamed x1 -> x0, local copies, waits for them, and re-layouts: 2.06 us -> none
    pallas_call x1, Pallas kernels: 33 us -> 31.6 us  [body(): pl.pallas_call(functools.partial(kernel, chips, steps), out_shape=jax.Sha...]
where the time goes in v3:
time: 56.8 us; the launch traced here: 56.6 us
  Pallas kernels  56.6 us (100%)
    pallas_call x1, Pallas kernels, body(): pl.pallas_call(functools.partial(kernel, chips, steps), out_shape=jax.Sha...  31.6 us
    pallas_call x1, Pallas kernels, body(): pl.pallas_call(handed_on, out_shape=jax.ShapeDtypeStruct(made.shape, BF16...  25 us

profile of v3, /device:TPU:12, one launch (start us, length us, event | category | flops | bytes accessed | tf_op | source)
XLA Modules:
  0.0 56.6 jit_solution(5494280236714290865)
XLA Ops:
  0.0 31.6 %shard_map.109.source = bf16[2,4,192,192]{3,2,1,0:T(8,128)(2,1)} custom-call(bf16[1,2,96,384]{3,2,1,0:T(8,128)(2,1)} %frames.1, bf16[2,2,96,384]{3,2,1,0:T(8,128)(2,1)} %cache.1, bf16[384]{0:T(512)(128)(2,1)} %gain.1, bf16[384,1152]{1,0:T(8,128)(2,1)} %wqkv_h.1, bf16[1152]{0:T(1024)(128)(2,1)} %bqkv.1, bf16[384,384]{1,0:T(8,128)(2,1)} %wproj_h.1, ...), custom_call_target="tpu_custom_call" | custom-call | flops 2000000000 | bytes 6000000 | tf_op jit(solution)/shard_map/pallas_call | solution.py:392
  31.6 25.0 %shard_map.110 = bf16[2,4,192,192]{3,2,1,0:T(8,128)(2,1)} custom-call(bf16[2,4,192,192]{3,2,1,0:T(8,128)(2,1)} %shard_map.109.source), custom_call_target="tpu_custom_call" | custom-call | tf_op jit(solution)/shard_map/pallas_call | solution.py:433

commit v4 on v3

--- a/solution.py
+++ b/solution.py
@@ -365,16 +365,19 @@
         give(j).wait()
 
 
-def handed_on(source, target, sem):
-    moves = [
-        pltpu.make_async_copy(source.at[f, j], target.at[f, j], sem.at[f, j])
-        for f in range(2)
-        for j in range(4)
+def handed_on(source, target, held, into, out):
+    places = [(f, j) for f in range(2) for j in range(4)]
+    comes = [
+        pltpu.make_async_copy(source.at[f, j], held.at[f, j], into.at[f, j]) for f, j in places
     ]
-    for move in moves:
-        move.start()
-    for move in moves:
-        move.wait()
+    goes = [pltpu.make_async_copy(held.at[f, j], target.at[f, j], out.at[f, j]) for f, j in places]
+    for come in comes:
+        come.start()
+    for come, go in zip(comes, goes):
+        come.wait()
+        go.start()
+    for go in goes:
+        go.wait()
 
 
 def solution(mesh):
@@ -435,7 +438,7 @@
             out_shape=jax.ShapeDtypeStruct(made.shape, BF16),
             in_specs=[away],
             out_specs=away,
-            scratch_shapes=[dma((2, 4))],
+            scratch_shapes=[pltpu.VMEM(made.shape, BF16), dma((2, 4)), dma((2, 4))],
             compiler_params=pltpu.CompilerParams(vmem_limit_bytes=60 * 2**20),
         )(made)
 

time: 56.8 us -> 33.8 us (0.60)
  Pallas kernels: 56.6 us -> 33.6 us
    pallas_call x1, Pallas kernels: 25 us -> 1.99 us  [body(): pl.pallas_call(handed_on, out_shape=jax.ShapeDtypeStruct(made.shape, BF16...]
where the time goes in v4:
time: 33.8 us; the launch traced here: 33.6 us
  Pallas kernels  33.6 us (99%)
    pallas_call x1, Pallas kernels, body(): pl.pallas_call(functools.partial(kernel, chips, steps), out_shape=jax.Sha...  31.6 us
    pallas_call x1, Pallas kernels, body(): pl.pallas_call(handed_on, out_shape=jax.ShapeDtypeStruct(made.shape, BF16...  1.99 us

profile of v4, /device:TPU:12, one launch (start us, length us, event | category | flops | bytes accessed | tf_op | source)
XLA Modules:
  0.0 33.6 jit_solution(3112542530008283669)
XLA Ops:
  0.0 31.6 %shard_map.109.source = bf16[2,4,192,192]{3,2,1,0:T(8,128)(2,1)} custom-call(bf16[1,2,96,384]{3,2,1,0:T(8,128)(2,1)} %frames.1, bf16[2,2,96,384]{3,2,1,0:T(8,128)(2,1)} %cache.1, bf16[384]{0:T(512)(128)(2,1)} %gain.1, bf16[384,1152]{1,0:T(8,128)(2,1)} %wqkv_h.1, bf16[1152]{0:T(1024)(128)(2,1)} %bqkv.1, bf16[384,384]{1,0:T(8,128)(2,1)} %wproj_h.1, ...), custom_call_target="tpu_custom_call" | custom-call | flops 2000000000 | bytes 6000000 | tf_op jit(solution)/shard_map/pallas_call | solution.py:395
  31.6 2.0 %shard_map.110 = bf16[2,4,192,192]{3,2,1,0:T(8,128)(2,1)} custom-call(bf16[2,4,192,192]{3,2,1,0:T(8,128)(2,1)} %shard_map.109.source), custom_call_target="tpu_custom_call" | custom-call | tf_op jit(solution)/shard_map/pallas_call | solution.py:436

commit v5 on v4

--- a/solution.py
+++ b/solution.py
@@ -174,7 +174,7 @@
 
     loads[1].wait()
     groups = (((0,), (1, 2)), ((0, 1), (2,)))
-    for pr in range(2):
+    def fold(pr):
         for pc in range(2):
             for dr in range(2):
                 for dc in range(2):
@@ -187,9 +187,13 @@
                     wf[pr, pc, :c2, at : at + ch] = part.astype(BF16)
             wf[pr, pc, c2:, :] = jnp.zeros((256 - c2, 4 * ch), BF16)
 
+    fold(0)
     take(1)
-
-    @pl.loop(2, chips)
+    forward(2)
+    fold(1)
+    take(2)
+
+    @pl.loop(3, chips)
     def _(d):
         forward(d)
         take(d)

time: 33.8 us -> 34 us (level)
  no operation moved by 1% of the time
where the time goes in v5:
time: 34 us; the launch traced here: 33.8 us
  Pallas kernels  33.8 us (99%)
    pallas_call x1, Pallas kernels, body(): pl.pallas_call(functools.partial(kernel, chips, steps), out_shape=jax.Sha...  31.8 us
    pallas_call x1, Pallas kernels, body(): pl.pallas_call(handed_on, out_shape=jax.ShapeDtypeStruct(made.shape, BF16...  1.99 us

profile of v5, /device:TPU:12, one launch (start us, length us, event | category | flops | bytes accessed | tf_op | source)
XLA Modules:
  0.0 33.8 jit_solution(6269923480437791428)
XLA Ops:
  0.0 31.8 %shard_map.109.source = bf16[2,4,192,192]{3,2,1,0:T(8,128)(2,1)} custom-call(bf16[1,2,96,384]{3,2,1,0:T(8,128)(2,1)} %frames.1, bf16[2,2,96,384]{3,2,1,0:T(8,128)(2,1)} %cache.1, bf16[384]{0:T(512)(128)(2,1)} %gain.1, bf16[384,1152]{1,0:T(8,128)(2,1)} %wqkv_h.1, bf16[1152]{0:T(1024)(128)(2,1)} %bqkv.1, bf16[384,384]{1,0:T(8,128)(2,1)} %wproj_h.1, ...), custom_call_target="tpu_custom_call" | custom-call | flops 2000000000 | bytes 6000000 | tf_op jit(solution)/shard_map/pallas_call | solution.py:399
  31.8 2.0 %shard_map.110 = bf16[2,4,192,192]{3,2,1,0:T(8,128)(2,1)} custom-call(bf16[2,4,192,192]{3,2,1,0:T(8,128)(2,1)} %shard_map.109.source), custom_call_target="tpu_custom_call" | custom-call | tf_op jit(solution)/shard_map/pallas_call | solution.py:440

commit v6 on v4

--- a/solution.py
+++ b/solution.py
@@ -259,18 +259,19 @@
             device_id_type=MESH,
         )
 
+    @pl.when(t >= 2)
+    def _():
+        for h in range(2):
+            passed(h, 0, t - 2).wait_recv()
+
+    tacc[...] = tacc[...] + mm(hist[0].reshape(rows, ch), wtime[0])
+
     for r in range(2):
-        @pl.when(t >= 2)
-        def _(r=r):
-            passed(r, 0, t - 2).wait_recv()
-
         @pl.when(t >= 1)
         def _(r=r):
             passed(r, 1, t - 1).wait_recv()
 
-        row = (
-            tacc[pl.ds(r * width, width), :] + mm(hist[1, r], wtime[1]) + mm(hist[0, r], wtime[0])
-        ).astype(BF16)
+        row = (tacc[pl.ds(r * width, width), :] + mm(hist[1, r], wtime[1])).astype(BF16)
         tim[r] = row
         goes = (s > 0) if r == 0 else (s < n_space - 1)
 

time: 33.8 us -> 34.3 us (1.015)
  Pallas kernels: 33.6 us -> 34.1 us
    pallas_call x1, Pallas kernels: 31.6 us -> 32.1 us  [body(): pl.pallas_call(functools.partial(kernel, chips, steps), out_shape=jax.Sha...]
where the time goes in v6:
time: 34.3 us; the launch traced here: 34.1 us
  Pallas kernels  34.1 us (99%)
    pallas_call x1, Pallas kernels, body(): pl.pallas_call(functools.partial(kernel, chips, steps), out_shape=jax.Sha...  32.1 us
    pallas_call x1, Pallas kernels, body(): pl.pallas_call(handed_on, out_shape=jax.ShapeDtypeStruct(made.shape, BF16...  1.99 us

profile of v6, /device:TPU:12, one launch (start us, length us, event | category | flops | bytes accessed | tf_op | source)
XLA Modules:
  0.0 34.1 jit_solution(17745279331430975444)
XLA Ops:
  0.0 32.1 %shard_map.109.source = bf16[2,4,192,192]{3,2,1,0:T(8,128)(2,1)} custom-call(bf16[1,2,96,384]{3,2,1,0:T(8,128)(2,1)} %frames.1, bf16[2,2,96,384]{3,2,1,0:T(8,128)(2,1)} %cache.1, bf16[384]{0:T(512)(128)(2,1)} %gain.1, bf16[384,1152]{1,0:T(8,128)(2,1)} %wqkv_h.1, bf16[1152]{0:T(1024)(128)(2,1)} %bqkv.1, bf16[384,384]{1,0:T(8,128)(2,1)} %wproj_h.1, ...), custom_call_target="tpu_custom_call" | custom-call | flops 2000000000 | bytes 6000000 | tf_op jit(solution)/shard_map/pallas_call | solution.py:396
  32.1 2.0 %shard_map.110 = bf16[2,4,192,192]{3,2,1,0:T(8,128)(2,1)} custom-call(bf16[2,4,192,192]{3,2,1,0:T(8,128)(2,1)} %shard_map.109.source), custom_call_target="tpu_custom_call" | custom-call | tf_op jit(solution)/shard_map/pallas_call | solution.py:437
